TPU v7x, 32 devices: a whole 2x2x4 slice. The times are simulated.
32 devices in a mesh: grp: 4 (over x, core), seq: 8 (over z, y).
Axes of the slice: x: 2, y: 2, z: 4, core: 2. Of those that a mesh axis runs over, the one named last changes fastest.
Arguments:
- prompt_hidden: bfloat16 [16384, 7168], P(('grp', 'seq')), may hold values from -6 to 6
- decode_hidden: bfloat16 [2, 256, 7168], P(None, 'grp', 'seq'), may hold values from -6 to 6
- w_down: bfloat16 [7168, 2112], P('seq'), may hold values from -0.0625 to 0.0625
- kv_gain: float32 [512], replicated, may hold values from 0.1 to 1.9
- q_gain: float32 [1536], replicated, may hold values from 0.1 to 1.9
- w_uq: bfloat16 [1536, 12288], P(None, 'seq'), may hold values from -0.15625 to 0.15625
- w_uk: bfloat16 [64, 128, 512], P('seq'), may hold values from -0.5 to 0.5
- w_uv: bfloat16 [64, 512, 128], P('seq'), may hold values from -0.25 to 0.25
- w_out: bfloat16 [8192, 7168], P('seq'), may hold values from -0.09375 to 0.09375
- cache_lat: bfloat16 [256, 64, 576], P('grp')
- cache_len: int32 [256], replicated, may hold values from 2 to 64, as said below
- prompt_route: int32 [4], replicated, may hold values from 0 to 3, as said below
- row_slot: int32 [4, 4096], replicated, may hold values from 0 to 4095, as said below
Outputs:
- decoded: bfloat16 [2, 256, 7168], P(None, 'grp', 'seq')
Inputs may be any that keep to these rules, and one draw needn't show every extreme that they name: `prompt_route`: a permutation: each decode group receives exactly one prefill group. Each row row_slot[g] is a permutation of 0 to 4095 that moves aligned pages of 8 rows whole, keeping the order inside a page. `cache_len`: every decode group has a sequence with 64 live rows.
All inputs are finite; a program needn't handle non-finite values.
Results may differ from a plain program's by a relative error of at most 0.025.
The roundings to bfloat16 on the way count: a program that leaves them out, or rounds other values in their place, can miss the bound.
Values may be sent and summed in bfloat16 or wider, within the bound.
No kernel may reach another device: no remote copies, remote signals or barrier semaphores. Data moves between devices by JAX's collectives and lax.ppermute only.
A program may use at most 128 MiB of HBM per device.

v0:
```python
import math

import jax
import jax.numpy as jnp
from jax import lax
from jax.sharding import PartitionSpec as P


def rms_norm(values, gain):
    return values * lax.rsqrt(jnp.mean(values * values, axis=-1, keepdims=True) + 1e-06) * gain


def rotate_half(values, positions):
    half = values.shape[-1] // 2
    ladder = jnp.arange(half, dtype=jnp.float32)
    freq = jnp.exp(ladder * (-2.0 * math.log(10000.0) / values.shape[-1]))
    angle = positions.astype(jnp.float32)[..., None] * freq
    cosine = jnp.cos(angle)
    sine = jnp.sin(angle)
    first_half = values[..., :half]
    second_half = values[..., half:]
    return jnp.concatenate(
        [first_half * cosine - second_half * sine, second_half * cosine + first_half * sine],
        axis=-1,
    )


def make_key(latent, gain, positions):
    width = gain.shape[0]
    normed = rms_norm(latent[..., :width], gain)
    turned = rotate_half(latent[..., width:], positions)
    return jnp.concatenate([normed, turned], axis=-1).astype(jnp.bfloat16)


def local(
    prompt_hidden,
    decode_hidden,
    w_down,
    kv_gain,
    q_gain,
    w_uq,
    w_uk,
    w_uv,
    w_out,
    cache_lat,
    cache_len,
    prompt_route,
    row_slot,
):
    seq_count = lax.axis_size("seq")
    group_count = lax.axis_size("grp")
    seq_index = lax.axis_index("seq")
    group_index = lax.axis_index("grp")
    token_count = prompt_hidden.shape[0]
    width_share = w_down.shape[0]
    q_width = q_gain.shape[0]
    kv_width = kv_gain.shape[0]
    latent_width = w_down.shape[1] - q_width
    kv_weight = w_down[:, q_width:]
    batch = cache_lat.shape[0]
    block_total = token_count * seq_count
    extra = block_total // batch
    spread = lax.all_to_all(prompt_hidden, "seq", split_axis=1, concat_axis=0, tiled=True)
    latent = lax.psum_scatter(
        jnp.dot(spread, kv_weight, preferred_element_type=jnp.float32),
        "seq",
        scatter_dimension=0,
        tiled=True,
    )
    target = prompt_route[group_index]
    target_lens = lax.dynamic_slice_in_dim(cache_len, target * batch, batch, 0)
    own_slots = lax.dynamic_slice_in_dim(
        lax.dynamic_index_in_dim(row_slot, group_index, 0, keepdims=False),
        seq_index * token_count,
        token_count,
        0,
    )
    owner = own_slots // extra
    owner_len = jnp.sum(
        jnp.where(
            owner[:, None] == jnp.arange(batch, dtype=jnp.int32)[None, :], target_lens[None, :], 0
        ),
        axis=1,
    )
    positions = owner_len + own_slots % extra
    new_rows = make_key(latent, kv_gain, positions)
    source = jnp.sum(
        jnp.where(prompt_route == group_index, jnp.arange(group_count, dtype=jnp.int32), 0)
    )
    is_target = (jnp.arange(group_count, dtype=jnp.int32) == target)[:, None, None]
    outgoing = jnp.where(is_target, new_rows[None], jnp.zeros_like(new_rows)[None])
    incoming = lax.all_to_all(outgoing, "grp", split_axis=0, concat_axis=0, tiled=True)
    chosen = lax.dynamic_index_in_dim(incoming, source, 0, keepdims=False)
    block_rows = lax.all_gather(chosen, "seq", axis=0, tiled=True)
    slots = lax.dynamic_index_in_dim(row_slot, source, 0, keepdims=False)
    arrival = (
        jnp.zeros_like(block_rows).at[slots].set(block_rows).reshape(batch, extra, latent_width)
    )
    local_len = lax.dynamic_slice_in_dim(cache_len, group_index * batch, batch, 0)
    steps = decode_hidden.shape[0]
    flat_hidden = decode_hidden.reshape(steps * batch, width_share)
    partial_down = jnp.dot(flat_hidden, w_down, preferred_element_type=jnp.float32)
    down = lax.psum(partial_down, "seq").reshape(steps, batch, -1)
    step_index = jnp.arange(steps, dtype=jnp.int32)
    dec_positions = local_len[None, :] + extra + step_index[:, None]
    q_latent = rms_norm(down[..., :q_width], q_gain).astype(jnp.bfloat16)
    fresh = make_key(down[..., q_width:], kv_gain, dec_positions)
    head_count = w_uk.shape[0]
    nope_width = w_uk.shape[1]
    rope_width = latent_width - kv_width
    projected = jnp.dot(
        q_latent.reshape(steps * batch, q_width), w_uq, preferred_element_type=jnp.float32
    )
    projected = projected.astype(jnp.bfloat16).reshape(
        steps, batch, head_count, nope_width + rope_width
    )
    absorbed = jnp.einsum(
        "tbhn,hnc->tbhc", projected[..., :nope_width], w_uk, preferred_element_type=jnp.float32
    )
    rotated = rotate_half(projected[..., nope_width:].astype(jnp.float32), dec_positions[..., None])
    queries = jnp.concatenate([absorbed, rotated], axis=-1).astype(jnp.bfloat16)
    key_rows = jnp.concatenate([cache_lat, arrival, jnp.transpose(fresh, (1, 0, 2))], axis=1)
    cache_size = cache_lat.shape[1]
    key_total = key_rows.shape[1]
    key_index = jnp.arange(key_total, dtype=jnp.int32)
    in_cache = key_index[None, None, :] < local_len[None, :, None]
    visible = jnp.where(
        (key_index < cache_size)[None, None, :],
        in_cache,
        jnp.where(
            (key_index == key_total - 1)[None, None, :], step_index[:, None, None] == 1, True
        ),
    )
    scores = jnp.einsum("tbhc,bkc->tbhk", queries, key_rows, preferred_element_type=jnp.float32) * (
        nope_width + rope_width
    ) ** (-0.5)
    scores = jnp.where(visible[:, :, None, :], scores, -1e30)
    highest = jnp.max(scores, axis=-1, keepdims=True)
    expo = jnp.exp(scores - highest)
    probs = (expo / jnp.sum(expo, axis=-1, keepdims=True)).astype(jnp.bfloat16)
    context = jnp.einsum(
        "tbhk,bkc->tbhc", probs, key_rows[..., :kv_width], preferred_element_type=jnp.float32
    ).astype(jnp.bfloat16)
    head_out = jnp.einsum(
        "tbhc,hcv->tbhv", context, w_uv, preferred_element_type=jnp.float32
    ).astype(jnp.bfloat16)
    head_out = head_out.reshape(steps * batch, -1)
    feature_share = w_out.shape[1] // seq_count
    partial_out = jnp.dot(head_out, w_out, preferred_element_type=jnp.float32)
    totals = lax.psum(partial_out, "seq")
    mine = lax.dynamic_slice_in_dim(totals, seq_index * feature_share, feature_share, 1)
    return mine.reshape(steps, batch, feature_share).astype(jnp.bfloat16)


def solution(mesh):
    in_specs = (
        P(("grp", "seq"), None),
        P(None, "grp", "seq"),
        P("seq", None),
        P(),
        P(),
        P(None, "seq"),
        P("seq", None, None),
        P("seq", None, None),
        P("seq", None),
        P("grp", None, None),
        P(),
        P(),
        P(),
    )
    out_specs = P(None, "grp", "seq")
    return jax.shard_map(local, mesh=mesh, in_specs=in_specs, out_specs=out_specs, check_vma=False)
```

profile of v0, /device:TPU:0, one launch (start us, length us, event | category | flops | bytes accessed | tf_op | source)
XLA Modules:
  0.0 786.1 jit_solution(12695294062120641514)
XLA Ops:
  6.5 10.5 %copy.74 = bf16[512,7168]{0,1:T(8,128)(2,1)} copy(bf16[512,7168]{1,0:T(8,128)(2,1)} %param.13) | data formatting | bytes 14680064 | tf_op args[0]
  17.0 168.0 %all_to_all.24 = bf16[512,8,896]{0,2,1:T(8,128)(2,1)} all-to-all(bf16[512,8,896]{0,2,1:T(8,128)(2,1)} %bitcast.73), channel_id=1, replica_groups=mesh['grp'=4,'seq'=8] {'seq'}, dimensions={1} | all-to-all | bytes 14680064 | tf_op jit(solution)/shard_map/all_to_all | solution.py:63
  185.0 11.4 %copy.75 = bf16[8,512,896]{2,1,0:T(8,128)(2,1)} copy(bf16[8,512,896]{1,2,0:T(8,128)(2,1)} %bitcast.72) | data formatting | bytes 14680064 | tf_op jit(solution)/shard_map/all_to_all | solution.py:63
  196.5 9.8 %fusion.27 = f32[4096,576]{0,1:T(8,128)} fusion(bf16[4096,896]{1,0:T(8,128)(2,1)} %bitcast.76, bf16[896,2112]{0,1:T(8,128)(2,1)} %param.15), kind=kOutput, calls=%fused_computation.32 | convolution fusion | flops 4227858432 | bytes 17809408 | tf_op jit(solution)/shard_map/dot_general | solution.py:65
  209.8 159.1 %reduce-scatter.2.cloned.1.call-done = f32[512,576]{0,1:T(8,128)} async-done(((f32[4096,576]{0,1:T(8,128)}), f32[512,576]{0,1:T(8,128)}) %reduce-scatter.2.cloned.1.call-update) | async-done | bytes 1179664 | tf_op jit(solution)/shard_map/reduce_scatter | solution.py:64
  374.6 4.5 all-to-all-start.1
  379.1 3.3 fusion.51
  382.4 1.9 copy.78
  387.1 20.5 %all-to-all-done.1 = bf16[4,512,576]{1,2,0:T(8,128)(2,1)} async-done(((bf16[4,512,576]{1,2,0:T(8,128)(2,1)}), bf16[4,512,576]{1,2,0:T(8,128)(2,1)}, u32[]{:S(2)}, u32[]{:S(2)}) %all-to-all-start.1) | async-done | bytes 2359328 | tf_op jit(solution)/shard_map/all_to_all | solution.py:92
  407.6 1.9 constant_dynamic-slice_fusion
  412.0 75.1 %all-reduce.3.cloned.1.call-done = f32[2,64,2112]{1,2,0:T(8,128)} async-done(((f32[2,64,2112]{1,2,0:T(8,128)}), f32[2,64,2112]{1,2,0:T(8,128)}) %all-reduce.3.cloned.1.call-update) | async-done | bytes 1081360 | tf_op jit(solution)/shard_map/psum | solution.py:103
  488.7 2.6 multiply_convert_fusion
  491.2 2.3 copy.80
  493.5 4.0 convolution_convert_fusion
  497.6 2.3 reshape.298
  499.8 1.7 slice.70
  509.4 60.5 %all-gather.3.cloned.1.call-done = bf16[1,4096,576]{1,2,0:T(8,128)(2,1)} async-done(((bf16[1,512,576]{1,2,0:T(8,128)(2,1)}), bf16[1,4096,576]{1,2,0:T(8,128)(2,1)}) %all-gather.3.cloned.1.call-update) | async-done | bytes 4718608 | tf_op jit(solution)/shard_map/all_gather | solution.py:94
  569.9 7.6 copy.76
  577.5 22.0 %scatter_custom_fusion = bf16[4096,576]{1,0:T(8,128)(2,1)} fusion(s32[4096]{0:T(1024)} %bitcast.84, bf16[4096,576]{1,0:T(8,128)(2,1)} %copy.76, bf16[]{:T(256)} %constant.78.clone.1), kind=kCustom, calls=%fused_computation.7 | custom fusion | bytes 4719104 | tf_op jit(solution)/shard_map/scatter | solution.py:97
  599.5 10.9 %pad_maximum_fusion = bf16[64,130,576]{2,1,0:T(8,128)(2,1)} fusion(bf16[64,2,576]{2,1,0:T(2,128)(2,1)S(1)} %copy.79, bf16[64,64,576]{2,1,0:T(8,128)(2,1)} %bitcast.74, bf16[64,64,576]{2,1,0:T(8,128)(2,1)} %param.22), kind=kLoop, calls=%fused_computation.2 | loop fusion | flops 28753920 | bytes 19169280 | tf_op jit(solution)/shard_map/concatenate | solution.py:122
  610.5 7.2 fusion.46
  617.7 5.0 fusion.8
  624.1 9.1 %fusion.30 = f32[128,7168]{1,0:T(8,128)} fusion(bf16[1024,7168]{1,0:T(8,128)(2,1)} %param.21, bf16[16,8,8,128]{3,2,1,0:T(8,128)(2,1)S(1)} %bitcast.80), kind=kOutput, calls=%fused_computation.42 | convolution fusion | flops 1879048192 | bytes 18612224 | tf_op jit(solution)/shard_map/dot_general | solution.py:149
  633.3 145.6 %all-reduce.4 = bf16[128,7168]{1,0:T(8,128)(2,1)S(1)} all-reduce(f32[128,7168]{1,0:T(8,128)} %fusion.30), channel_id=1, replica_groups=mesh['grp'=4,'seq'=8] {'seq'}, use_global_device_ids=true, to_apply=%region_10.11 | all-reduce | flops 917504 | bytes 5505024 | tf_op jit(solution)/shard_map/psum | solution.py:150
  (68 shorter events, 23.4 us)
Async XLA Ops:
  6.5 502.1 %copy-start = (bf16[8,128,512]{2,1,0:T(8,128)(2,1)S(1)}, bf16[8,128,512]{2,1,0:T(8,128)(2,1)}, u32[]{:S(2)}) copy-start(bf16[8,128,512]{2,1,0:T(8,128)(2,1)} %param.19) | copy-start | bytes 3145732
  6.5 362.4 %reduce-scatter.2.cloned.1.call-start = ((), (), s32[]{:S(2)}) async-start(), calls=%async_computation.3 | async-start | bytes 10616832 | tf_op jit(solution)/shard_map/reduce_scatter | solution.py:64
  206.2 0.7 copy-start.9
  206.2 3.4 copy-start.7
  206.2 165.2 %copy-start.6 = (f32[512]{0:T(512)S(1)}, f32[512]{0:T(512)}, u32[]{:S(2)}) copy-start(f32[512]{0:T(512)} %param.16) | copy-start | bytes 6148
  372.8 6.3 copy-start.3
  374.6 33.1 %all-to-all-start.1 = ((bf16[4,512,576]{1,2,0:T(8,128)(2,1)}), bf16[4,512,576]{1,2,0:T(8,128)(2,1)}, u32[]{:S(2)}, u32[]{:S(2)}) async-start(bf16[4,512,576]{1,2,0:T(8,128)(2,1)} %broadcast_select_fusion), calls=%async_computation.2 | async-start | bytes 4718592 | tf_op jit(solution)/shard_map/all_to_all | solution.py:92
  379.0 108.0 %all-reduce.3.cloned.1.call-start = ((), (), s32[]{:S(2)}) async-start(), calls=%async_computation.4 | async-start | bytes 4325376 | tf_op jit(solution)/shard_map/psum | solution.py:103
  382.4 106.2 %copy-start.5 = (f32[1536]{0:T(1024)S(1)}, f32[1536]{0:T(1024)}, u32[]{:S(2)}) copy-start(f32[1536]{0:T(1024)} %param.17) | copy-start | bytes 18436
  384.3 185.5 %all-gather.3.cloned.1.call-start = ((), (), s32[]{:S(2)}) async-start(), calls=%async_computation.5 | async-start | bytes 5308416 | tf_op jit(solution)/shard_map/all_gather | solution.py:94
  491.2 10.3 %copy-start.2 = (f32[2,64,2112]{1,2,0:T(8,128)S(1)}, f32[2,64,2112]{1,2,0:T(8,128)}, u32[]{:S(2)}) copy-start(f32[2,64,2112]{1,2,0:T(8,128)} %all-reduce.3.cloned.1.call-done) | copy-start | bytes 3244036
  499.8 8.9 %slice-start = ((bf16[2,64,8,192]{3,2,1,0:T(8,128)(2,1)}), bf16[2,64,8,128]{3,2,1,0:T(8,128)(2,1)S(1)}, s32[]{:S(2)}) async-start(bf16[2,64,8,192]{3,2,1,0:T(8,128)(2,1)} %reshape.298), calls=%async_computation.6 | async-start | bytes 524288 | tf_op jit(solution)/shard_map/slice | solution.py:118
  599.5 11.0 %copy-start.4 = (pred[2,64,130]{2,0,1:T(4,128)(4,1)S(1)}, pred[2,64,130]{2,0,1:T(4,128)(4,1)}, u32[]{:S(2)}) copy-start(pred[2,64,130]{2,0,1:T(4,128)(4,1)} %broadcast_select_fusion.1) | copy-start | bytes 49924
  617.6 5.0 copy-start.8
  624.1 155.5 %copy-start.1 = (bf16[8,128,512]{2,1,0:T(8,128)(2,1)S(1)}, bf16[8,128,512]{2,1,0:T(8,128)(2,1)}, u32[]{:S(2)}) copy-start(bf16[8,128,512]{2,1,0:T(8,128)(2,1)} %param.19) | copy-start | bytes 3145732
Sparse Core Ops, SparseCore 0:
  206.4 162.4 reduce-scatter.1
  384.5 102.5 all-reduce.2
  489.1 80.7 all-gather.2
where the time goes:
time: 788 us; the launch traced here: 786 us
  waiting for transfers between devices  315 us (40%)
  blocking collectives  314 us (40%)
  local copies, waits for them, and re-layouts  67 us (9%)
  matrix products  40.1 us (5%)
  other arithmetic  29.4 us (4%)
  between operations  16 us (2%)
    all_to_all x1, blocking collectives, local(): lax.all_to_all(prompt_hidden, 'seq', split_axis=1, concat_axis=0, tiled=T...  168 us
    reduce_scatter x1, waiting for transfers between devices, local(): lax.psum_scatter(jnp.dot(spread, kv_weight, preferred_element_type=jnp.fl...  159 us
    psum x1, blocking collectives, local(): totals = lax.psum(partial_out, 'seq')  146 us
    psum x1, waiting for transfers between devices, local(): down = lax.psum(partial_down, 'seq').reshape(steps, batch, -1)  75.1 us
    all_gather x1, waiting for transfers between devices, local(): block_rows = lax.all_gather(chosen, 'seq', axis=0, tiled=True)  60.5 us
    scatter x1, local copies, waits for them, and re-layouts, local(): jnp.zeros_like(block_rows).at[slots].set(block_rows)  22 us
    all_to_all x1, waiting for transfers between devices, local(): lax.all_to_all(outgoing, 'grp', split_axis=0, concat_axis=0, tiled=True)  20.5 us
  transfers between devices with their start and end apart: 4, of which 4 were waited for; matrix products, arithmetic and copies ran while one was open for 4% of the time, Pallas kernels for 0%

commit v1 on v0

--- a/solution.py
+++ b/solution.py
@@ -4,6 +4,14 @@
 import jax.numpy as jnp
 from jax import lax
 from jax.sharding import PartitionSpec as P
+
+
+def ring_order(count):
+    if count == 16:
+        cells = [(0, 0), (0, 1), (0, 2), (0, 3), (1, 3), (1, 2), (1, 1), (2, 1)]
+        cells += [(2, 2), (2, 3), (3, 3), (3, 2), (3, 1), (3, 0), (2, 0), (1, 0)]
+        return [a * 4 + b for a, b in cells]
+    return list(range(0, count, 2)) + list(range(count - 1, 0, -2))
 
 
 def rms_norm(values, gain):
@@ -30,6 +38,64 @@
     normed = rms_norm(latent[..., :width], gain)
     turned = rotate_half(latent[..., width:], positions)
     return jnp.concatenate([normed, turned], axis=-1).astype(jnp.bfloat16)
+
+
+class Ring:
+    def __init__(self, count):
+        self.count = count
+        self.order = ring_order(count)
+        places = [0] * count
+        for place, index in enumerate(self.order):
+            places[index] = place
+        self.place = jnp.array(places, jnp.int32)[lax.axis_index("seq")]
+        nexts = self.order[1:] + self.order[:1]
+        self.forward = list(zip(self.order, nexts))
+        self.backward = [(b, a) for a, b in self.forward]
+
+    def member(self, offset):
+        return jnp.array(self.order, jnp.int32)[(self.place + offset) % self.count]
+
+    def send(self, value, forward):
+        return lax.ppermute(value, "seq", self.forward if forward else self.backward)
+
+    def gather(self, block):
+        half = self.count // 2
+        ahead = behind = block
+        for step in range(1, half):
+            ahead = self.send(ahead, True)
+            behind = self.send(behind, False)
+            yield self.member(-step), 0, ahead
+            yield self.member(step), 0, behind
+        cut = block.shape[0] // 2
+        last_ahead = self.send(ahead[:cut], True)
+        last_behind = self.send(behind[cut:], False)
+        yield self.member(half), 0, last_ahead
+        yield self.member(half), cut, last_behind
+
+    def reduce_scatter(self, part_of, columns):
+        half = self.count // 2
+        cut = columns // 2
+        far = part_of(self.member(half))
+        ahead = self.send(far[:, :cut].astype(jnp.bfloat16), True)
+        behind = self.send(far[:, cut:].astype(jnp.bfloat16), False)
+        for step in range(half - 1, 0, -1):
+            near_ahead = part_of(self.member(step))
+            near_behind = part_of(self.member(-step))
+            if step == half - 1:
+                near_ahead = jnp.concatenate(
+                    [near_ahead[:, :cut] + ahead.astype(jnp.float32), near_ahead[:, cut:]], axis=1
+                )
+                near_behind = jnp.concatenate(
+                    [near_behind[:, :cut], near_behind[:, cut:] + behind.astype(jnp.float32)],
+                    axis=1,
+                )
+            else:
+                near_ahead = near_ahead + ahead.astype(jnp.float32)
+                near_behind = near_behind + behind.astype(jnp.float32)
+            ahead = self.send(near_ahead.astype(jnp.bfloat16), True)
+            behind = self.send(near_behind.astype(jnp.bfloat16), False)
+        own = part_of(self.member(0))
+        return own + (ahead.astype(jnp.float32) + behind.astype(jnp.float32))
 
 
 def local(
@@ -56,17 +122,46 @@
     q_width = q_gain.shape[0]
     kv_width = kv_gain.shape[0]
     latent_width = w_down.shape[1] - q_width
-    kv_weight = w_down[:, q_width:]
     batch = cache_lat.shape[0]
     block_total = token_count * seq_count
     extra = block_total // batch
-    spread = lax.all_to_all(prompt_hidden, "seq", split_axis=1, concat_axis=0, tiled=True)
-    latent = lax.psum_scatter(
-        jnp.dot(spread, kv_weight, preferred_element_type=jnp.float32),
-        "seq",
-        scatter_dimension=0,
-        tiled=True,
-    )
+    steps = decode_hidden.shape[0]
+    core = group_index % 2
+    chip = group_index // 2
+    chips = group_count // 2
+    ring = Ring(seq_count)
+    swap_cores = [(g, g ^ 1) for g in range(group_count)]
+
+    kv_weight = w_down[:, q_width:]
+    share = width_share // 2
+    carried = lax.dynamic_slice_in_dim(kv_weight, core * share, share, 0)
+    weight = jnp.zeros((width_share * seq_count, latent_width), jnp.bfloat16)
+    weight = lax.dynamic_update_slice_in_dim(weight, kv_weight, seq_index * width_share, 0)
+    for member, start, rows in ring.gather(carried):
+        swapped = lax.ppermute(rows, "grp", swap_cores)
+        base = member * width_share + start
+        weight = lax.dynamic_update_slice_in_dim(weight, rows, base + core * share, 0)
+        weight = lax.dynamic_update_slice_in_dim(weight, swapped, base + (1 - core) * share, 0)
+
+    decode_rows = steps * batch
+    flat_hidden = decode_hidden.reshape(decode_rows, width_share)
+    partial_down = jnp.dot(flat_hidden, w_down, preferred_element_type=jnp.float32)
+    down = lax.psum_scatter(partial_down, "seq", scatter_dimension=0, tiled=True)
+    local_len = lax.dynamic_slice_in_dim(cache_len, group_index * batch, batch, 0)
+    own_rows = decode_rows // seq_count
+    own_index = seq_index * own_rows + jnp.arange(own_rows, dtype=jnp.int32)
+    own_positions = local_len[own_index % batch] + extra + own_index // batch
+    own_latent = jnp.concatenate(
+        [
+            rms_norm(down[:, :q_width], q_gain).astype(jnp.bfloat16),
+            make_key(down[:, q_width:], kv_gain, own_positions),
+        ],
+        axis=1,
+    )
+    latents = lax.all_gather(own_latent, "seq", axis=0, tiled=True)
+    q_latent = latents[:, :q_width]
+    fresh = latents[:, q_width:].reshape(steps, batch, latent_width)
+
     target = prompt_route[group_index]
     target_lens = lax.dynamic_slice_in_dim(cache_len, target * batch, batch, 0)
     own_slots = lax.dynamic_slice_in_dim(
@@ -75,42 +170,57 @@
         token_count,
         0,
     )
-    owner = own_slots // extra
     owner_len = jnp.sum(
         jnp.where(
-            owner[:, None] == jnp.arange(batch, dtype=jnp.int32)[None, :], target_lens[None, :], 0
+            (own_slots // extra)[:, None] == jnp.arange(batch, dtype=jnp.int32)[None, :],
+            target_lens[None, :],
+            0,
         ),
         axis=1,
     )
     positions = owner_len + own_slots % extra
+    latent = jnp.dot(prompt_hidden, weight, preferred_element_type=jnp.float32)
     new_rows = make_key(latent, kv_gain, positions)
-    source = jnp.sum(
-        jnp.where(prompt_route == group_index, jnp.arange(group_count, dtype=jnp.int32), 0)
-    )
-    is_target = (jnp.arange(group_count, dtype=jnp.int32) == target)[:, None, None]
-    outgoing = jnp.where(is_target, new_rows[None], jnp.zeros_like(new_rows)[None])
-    incoming = lax.all_to_all(outgoing, "grp", split_axis=0, concat_axis=0, tiled=True)
-    chosen = lax.dynamic_index_in_dim(incoming, source, 0, keepdims=False)
-    block_rows = lax.all_gather(chosen, "seq", axis=0, tiled=True)
+
+    groups = jnp.arange(group_count, dtype=jnp.int32)
+    sources = jnp.sum(
+        jnp.where(prompt_route[None, :] == groups[:, None], groups[None, :], 0), axis=1
+    )
+    source = sources[group_index]
+    other_rows = lax.ppermute(new_rows, "grp", swap_cores)
+    chosen = jnp.where(source % 2 == core, new_rows, other_rows)
+    for shift in range(1, chips):
+        reached = sources[((chip + shift) % chips) * 2 + core]
+        outgoing = jnp.where(reached % 2 == core, new_rows, other_rows)
+        incoming = lax.ppermute(
+            outgoing, "grp", [(g, (g + 2 * shift) % group_count) for g in range(group_count)]
+        )
+        chosen = jnp.where(source // 2 == (chip - shift) % chips, incoming, chosen)
+    block_rows = jnp.zeros((block_total, latent_width), jnp.bfloat16)
+    block_rows = lax.dynamic_update_slice_in_dim(block_rows, chosen, seq_index * token_count, 0)
+    for member, start, rows in ring.gather(chosen):
+        block_rows = lax.dynamic_update_slice_in_dim(
+            block_rows, rows, member * token_count + start, 0
+        )
+
+    page = 8
     slots = lax.dynamic_index_in_dim(row_slot, source, 0, keepdims=False)
-    arrival = (
-        jnp.zeros_like(block_rows).at[slots].set(block_rows).reshape(batch, extra, latent_width)
-    )
-    local_len = lax.dynamic_slice_in_dim(cache_len, group_index * batch, batch, 0)
-    steps = decode_hidden.shape[0]
-    flat_hidden = decode_hidden.reshape(steps * batch, width_share)
-    partial_down = jnp.dot(flat_hidden, w_down, preferred_element_type=jnp.float32)
-    down = lax.psum(partial_down, "seq").reshape(steps, batch, -1)
+    page_of = slots.reshape(-1, page)[:, 0] // page
+    pages = page_of.shape[0]
+    page_index = jnp.arange(pages, dtype=jnp.int32)
+    page_from = jnp.sum(
+        jnp.where(page_of[None, :] == page_index[:, None], page_index[None, :], 0), axis=1
+    )
+    arrival = block_rows.reshape(pages, page, latent_width)[page_from].reshape(
+        batch, extra, latent_width
+    )
+
     step_index = jnp.arange(steps, dtype=jnp.int32)
     dec_positions = local_len[None, :] + extra + step_index[:, None]
-    q_latent = rms_norm(down[..., :q_width], q_gain).astype(jnp.bfloat16)
-    fresh = make_key(down[..., q_width:], kv_gain, dec_positions)
     head_count = w_uk.shape[0]
     nope_width = w_uk.shape[1]
     rope_width = latent_width - kv_width
-    projected = jnp.dot(
-        q_latent.reshape(steps * batch, q_width), w_uq, preferred_element_type=jnp.float32
-    )
+    projected = jnp.dot(q_latent, w_uq, preferred_element_type=jnp.float32)
     projected = projected.astype(jnp.bfloat16).reshape(
         steps, batch, head_count, nope_width + rope_width
     )
@@ -144,12 +254,15 @@
     head_out = jnp.einsum(
         "tbhc,hcv->tbhv", context, w_uv, preferred_element_type=jnp.float32
     ).astype(jnp.bfloat16)
-    head_out = head_out.reshape(steps * batch, -1)
+    head_out = head_out.reshape(decode_rows, -1)
     feature_share = w_out.shape[1] // seq_count
-    partial_out = jnp.dot(head_out, w_out, preferred_element_type=jnp.float32)
-    totals = lax.psum(partial_out, "seq")
-    mine = lax.dynamic_slice_in_dim(totals, seq_index * feature_share, feature_share, 1)
-    return mine.reshape(steps, batch, feature_share).astype(jnp.bfloat16)
+
+    def part_of(member):
+        columns = lax.dynamic_slice_in_dim(w_out, member * feature_share, feature_share, 1)
+        return jnp.dot(head_out, columns, preferred_element_type=jnp.float32)
+
+    total = ring.reduce_scatter(part_of, feature_share)
+    return total.reshape(steps, batch, feature_share).astype(jnp.bfloat16)
 
 
 def solution(mesh):

time: 788 us -> 292 us (0.37)
  blocking collectives: 314 us -> 41.9 us
  waiting for transfers between devices: 315 us -> 62.7 us
  starting transfers between devices: 4.75 us -> 31.3 us
  between operations: 16 us -> 37.1 us
  local copies, waits for them, and re-layouts: 67 us -> 58.3 us
    all_to_all x1 -> x0, blocking collectives: 168 us -> none  [local(): lax.all_to_all(prompt_hidden, 'seq', split_axis=1, concat_axis=0, tiled=T...]
    reduce_scatter x1, waiting for transfers between devices: 159 us -> 0.01 us  [local(): lax.psum_scatter(partial_down, 'seq', scatter_dimension=0, tiled=True)]
    psum x1 -> x0, blocking collectives: 146 us -> none  [local(): totals = lax.psum(partial_out, 'seq')]
    psum x1 -> x0, waiting for transfers between devices: 75.1 us -> none  [local(): down = lax.psum(partial_down, 'seq').reshape(steps, batch, -1)]
    ppermute x0 -> x34, waiting for transfers between devices: none -> 62.7 us  [the longest x24 50.1 us: send(): lax.ppermute(value, 'seq', self.forward if forward else self.backward)]
    all_gather x1 -> x0, waiting for transfers between devices: 60.5 us -> none  [local(): block_rows = lax.all_gather(chosen, 'seq', axis=0, tiled=True)]
    all_gather x0 -> x1, blocking collectives: none -> 41.9 us  [local(): latents = lax.all_gather(own_latent, 'seq', axis=0, tiled=True)]
    ppermute x0 -> x34, starting transfers between devices: none -> 31.3 us  [the longest x24 27.3 us: send(): lax.ppermute(value, 'seq', self.forward if forward else self.backward)]
  transfers between devices with their start and end apart: 4 -> 35, of which waited for: 4 -> 17; matrix products, arithmetic and copies ran while one was open for 4% -> 27% of each run, Pallas kernels for 0% -> 0%
where the time goes in v1:
time: 292 us; the launch traced here: 291 us
  waiting for transfers between devices  62.7 us (21%)
  local copies, waits for them, and re-layouts  58.3 us (20%)
  blocking collectives  41.9 us (14%)
  matrix products  37.6 us (13%)
  between operations  37.1 us (13%)
  starting transfers between devices  31.3 us (11%)
  other arithmetic  21.9 us (8%)
    ppermute x24, waiting for transfers between devices, send(): lax.ppermute(value, 'seq', self.forward if forward else self.backward)  50.1 us
    all_gather x1, blocking collectives, local(): latents = lax.all_gather(own_latent, 'seq', axis=0, tiled=True)  41.9 us
    ppermute x24, starting transfers between devices, send(): lax.ppermute(value, 'seq', self.forward if forward else self.backward)  27.3 us
    ppermute x1, waiting for transfers between devices, local(): lax.ppermute(outgoing, 'grp', [(g, (g + 2 * shift) % group_count) for g i...  12.6 us
    concatenate x1, other arithmetic, local(): jnp.concatenate([cache_lat, arrival, jnp.transpose(fresh, (1, 0, 2))], ax...  11.1 us
    dynamic_update_slice x8, local copies, waits for them, and re-layouts, local(): lax.dynamic_update_slice_in_dim(weight, rows, base + core * share, 0)  9.94 us
    dynamic_update_slice x8, local copies, waits for them, and re-layouts, local(): lax.dynamic_update_slice_in_dim(weight, swapped, base + (1 - core) * shar...  9.46 us
    dot_general x8, matrix products, part_of(): return jnp.dot(head_out, columns, preferred_element_type=jnp.float32)  8.25 us
  transfers between devices with their start and end apart: 35, of which 17 were waited for; matrix products, arithmetic and copies ran while one was open for 27% of the time, Pallas kernels for 0%

profile of v1, /device:TPU:0, one launch (start us, length us, event | category | flops | bytes accessed | tf_op | source)
XLA Modules:
  0.0 290.8 jit_solution(7743157578856111160)
XLA Ops:
  10.0 3.0 %collective-permute-start = (bf16[448,576]{1,0:T(8,128)(2,1)}, bf16[448,576]{1,0:T(8,128)(2,1)}, u32[]{:S(2)}, u32[]{:S(2)}) collective-permute-start(bf16[448,576]{1,0:T(8,128)(2,1)} %constant_dynamic-slice_fusion), channel_id=1, source_target_pairs={{0,2},{2,4},{4,6},{6,7},{7,5},{5,3},{3,1},{1,0},{8,10},{10,12},{12... | collective-permute-start | bytes 1548296 | tf_op jit(solution)/shard_map/ppermute | solution.py:59
  13.0 4.4 %fusion.112 = f32[128,2112]{1,0:T(8,128)} fusion(bf16[128,896]{1,0:T(8,128)(2,1)S(1)} %bitcast.124, bf16[896,2112]{0,1:T(8,128)(2,1)} %param.40), kind=kOutput, calls=%fused_computation.201 | convolution fusion | flops 484442112 | bytes 5095424 | tf_op jit(solution)/shard_map/dot_general | solution.py:148
  29.6 4.3 %broadcast_in_dim.99 = bf16[7168,576]{1,0:T(8,128)(2,1)} broadcast(bf16[]{:T(256)} %constant.254.clone.1), dimensions={} | broadcast | bytes 8257538 | tf_op jit(solution)/shard_map/broadcast_in_dim | solution.py:138
  44.2 3.2 %collective-permute-done.4 = bf16[448,576]{1,0:T(8,128)(2,1)} collective-permute-done((bf16[448,576]{1,0:T(8,128)(2,1)}, bf16[448,576]{1,0:T(8,128)(2,1)}, u32[]{:S(2)}, u32[]{:S(2)}) %collective-permute-start.4) | collective-permute-done | bytes 516128 | tf_op jit(solution)/shard_map/ppermute | solution.py:59
  47.3 2.5 collective-permute-start.8
  68.8 2.5 constant_dynamic-update-slice_fusion.21
  74.6 6.1 %collective-permute-done.10 = bf16[448,576]{1,0:T(8,128)(2,1)S(1)} collective-permute-done((bf16[448,576]{1,0:T(8,128)(2,1)}, bf16[448,576]{1,0:T(8,128)(2,1)S(1)}, u32[]{:S(2)}, u32[]{:S(2)}) %collective-permute-start.10) | collective-permute-done | bytes 516128 | tf_op jit(solution)/shard_map/ppermute | solution.py:59
  80.6 2.4 collective-permute-start.14
  88.1 2.4 collective-permute-done.14
  96.1 7.9 %convolution_bitcast_fusion = f32[512,576]{0,1:T(8,128)S(1)} fusion(bf16[7168,576]{1,0:T(8,128)(2,1)} %constant_dynamic-update-slice_fusion.9, bf16[512,7168]{1,0:T(8,128)(2,1)S(1)} %bitcast.130), kind=kOutput, calls=%fused_computation.28 | convolution fusion | flops 4227858432 | bytes 16777216 | tf_op jit(solution)/shard_map/dot_general | solution.py:182
  111.9 12.6 %collective-permute-done.17 = bf16[512,576]{0,1:T(8,128)(2,1)S(1)} collective-permute-done((bf16[512,576]{0,1:T(8,128)(2,1)S(1)}, bf16[512,576]{0,1:T(8,128)(2,1)S(1)}, u32[]{:S(2)}, u32[]{:S(2)}) %collective-permute-start.17) | collective-permute-done | bytes 589856 | tf_op jit(solution)/shard_map/ppermute | solution.py:195
  126.3 41.9 %all_gather.3 = bf16[128,2112]{1,0:T(8,128)(2,1)S(1)} all-gather(bf16[16,2112]{1,0:T(8,128)(2,1)S(1)} %concatenate.26), channel_id=1, replica_groups=mesh['grp'=4,'seq'=8] {'seq'}, dimensions={0}, use_global_device_ids=true | all-gather | bytes 608256 | tf_op jit(solution)/shard_map/all_gather | solution.py:161
  168.6 3.1 %convolution_convert_fusion = bf16[128,1536]{1,0:T(8,128)(2,1)S(1)} fusion(bf16[1536,1536]{1,0:T(8,128)(2,1)} %param.43, bf16[128,2112]{1,0:T(8,128)(2,1)S(1)} %all_gather.3), kind=kOutput, calls=%fused_computation.8 | convolution fusion | flops 604176384 | bytes 5505024 | tf_op jit(solution)/shard_map/dot_general | solution.py:223
  174.1 8.3 %collective-permute-done.19 = bf16[512,576]{0,1:T(8,128)(2,1)} collective-permute-done((bf16[512,576]{0,1:T(8,128)(2,1)S(1)}, bf16[512,576]{0,1:T(8,128)(2,1)}, u32[]{:S(2)}, u32[]{:S(2)}) %collective-permute-start.19) | collective-permute-done | bytes 589856 | tf_op jit(solution)/shard_map/ppermute | solution.py:59
  183.4 3.8 %collective-permute-done.20 = bf16[512,576]{0,1:T(8,128)(2,1)} collective-permute-done((bf16[512,576]{0,1:T(8,128)(2,1)}, bf16[512,576]{0,1:T(8,128)(2,1)}, u32[]{:S(2)}, u32[]{:S(2)}) %collective-permute-start.20) | collective-permute-done | bytes 589856 | tf_op jit(solution)/shard_map/ppermute | solution.py:59
  190.3 7.5 %collective-permute-done.21 = bf16[512,576]{0,1:T(8,128)(2,1)} collective-permute-done((bf16[512,576]{0,1:T(8,128)(2,1)}, bf16[512,576]{0,1:T(8,128)(2,1)}, u32[]{:S(2)}, u32[]{:S(2)}) %collective-permute-start.21) | collective-permute-done | bytes 589856 | tf_op jit(solution)/shard_map/ppermute | solution.py:59
  197.8 2.7 broadcast_in_dim.92
  220.3 6.2 %gather_fusion = bf16[512,8,576]{2,1,0:T(8,128)(2,1)} fusion(bf16[512,8,576]{2,1,0:T(8,128)(2,1)} %bitcast.23, s32[1024]{0:T(1024)S(1)} %pad_clamp_fusion.1), kind=kCustom, calls=%fused_computation | custom fusion | bytes 9439232 | tf_op jit(solution)/shard_map/gather | solution.py:214
  226.5 11.1 %pad_maximum_fusion = bf16[64,130,576]{2,1,0:T(8,128)(2,1)} fusion(bf16[64,2,576]{2,1,0:T(2,128)(2,1)S(1)} %bitcast.121, bf16[64,64,576]{2,1,0:T(8,128)(2,1)} %bitcast.117, bf16[64,64,576]{2,1,0:T(8,128)(2,1)} %param.47), kind=kLoop, calls=%fused_computation.3 | loop fusion | flops 28753920 | bytes 19169280 | tf_op jit(solution)/shard_map/concatenate | solution.py:232
  237.6 7.2 %fusion.107 = (f32[2,64,8]{2,0,1:T(2,128)S(1)}, f32[2,64,8,130]{3,2,0,1:T(8,128)S(1)}) fusion(bf16[2,64,8,576]{3,1,0,2:T(8,128)(2,1)S(1)} %copy-done.2, pred[2,64,130]{2,0,1:T(4,128)(4,1)S(1)} %copy-done.6, bf16[64,2,576]{2,1,0:T(2,128)(2,1)S(1)} %bitcast.122, bf16[64,64,576]{2,1,0:T(8,128)(2,1)} %bitcast.118, bf16[64,64,576]{2,1,0:T(8,128)(2,1)} %param.47), kind=kOutput, calls=%fused_computation.200 | convolution fusion | flops 182640768 | bytes 11317504 | tf_op jit(solution)/shard_map/sub | solution.py:249
  244.8 5.0 %fusion.22 = bf16[2,64,8,512]{3,2,0,1:T(8,128)(2,1)S(1)} fusion(bf16[64,130,576]{2,1,0:T(8,128)(2,1)} %pad_maximum_fusion, f32[2,64,8,130]{3,2,0,1:T(8,128)S(1)} %get-tuple-element.29, f32[2,64,8]{2,0,1:T(2,128)S(1)} %get-tuple-element.28), kind=kOutput, calls=%fused_computation.29 | convolution fusion | flops 137105408 | bytes 10498048 | tf_op jit(solution)/shard_map/tbhk,bkc->tbhc/dot_general | solution.py:251
  265.1 3.3 %collective-permute-done.27 = bf16[128,896]{1,0:T(8,128)(2,1)S(1)} collective-permute-done((bf16[128,896]{1,0:T(8,128)(2,1)S(1)}, bf16[128,896]{1,0:T(8,128)(2,1)S(1)}, u32[]{:S(2)}, u32[]{:S(2)}) %collective-permute-start.27) | collective-permute-done | bytes 229408 | tf_op jit(solution)/shard_map/ppermute | solution.py:59
  271.6 3.3 %collective-permute-done.28 = bf16[128,896]{1,0:T(8,128)(2,1)S(1)} collective-permute-done((bf16[128,896]{1,0:T(8,128)(2,1)S(1)}, bf16[128,896]{1,0:T(8,128)(2,1)S(1)}, u32[]{:S(2)}, u32[]{:S(2)}) %collective-permute-start.28) | collective-permute-done | bytes 229408 | tf_op jit(solution)/shard_map/ppermute | solution.py:59
  278.2 2.8 collective-permute-done.29
  (214 shorter events, 96.3 us)
Async XLA Ops:
  6.5 98.8 %reduce-scatter.2.cloned.1.call-start = ((), (), s32[]{:S(2)}) async-start(), calls=%async_computation.1 | async-start | bytes 1253376 | tf_op jit(solution)/shard_map/reduce_scatter | solution.py:149
  10.0 16.3 %collective-permute-start = (bf16[448,576]{1,0:T(8,128)(2,1)}, bf16[448,576]{1,0:T(8,128)(2,1)}, u32[]{:S(2)}, u32[]{:S(2)}) collective-permute-start(bf16[448,576]{1,0:T(8,128)(2,1)} %constant_dynamic-slice_fusion), channel_id=1, source_target_pairs={{0,2},{2,4},{4,6},{6,7},{7,5},{5,3},{3,1},{1,0},{8,10},{10,12},{12... | collective-permute-start | bytes 1548296 | tf_op jit(solution)/shard_map/ppermute | solution.py:59
  13.0 15.0 %collective-permute-start.2 = (bf16[448,576]{1,0:T(8,128)(2,1)}, bf16[448,576]{1,0:T(8,128)(2,1)S(1)}, u32[]{:S(2)}, u32[]{:S(2)}) collective-permute-start(bf16[448,576]{1,0:T(8,128)(2,1)} %constant_dynamic-slice_fusion), channel_id=1, source_target_pairs={{2,0},{4,2},{6,4},{7,6},{5,7},{3,5},{1,3},{0,1},{10,8},{12,10},{14... | collective-permute-start | bytes 1548296 | tf_op jit(solution)/shard_map/ppermute | solution.py:59
  26.2 21.1 %collective-permute-start.4 = (bf16[448,576]{1,0:T(8,128)(2,1)}, bf16[448,576]{1,0:T(8,128)(2,1)}, u32[]{:S(2)}, u32[]{:S(2)}) collective-permute-start(bf16[448,576]{1,0:T(8,128)(2,1)} %collective-permute-done), channel_id=1, source_target_pairs={{0,2},{2,4},{4,6},{6,7},{7,5},{5,3},{3,1},{1,0},{8,10},{10,12},{12... | collective-permute-start | bytes 1548296 | tf_op jit(solution)/shard_map/ppermute | solution.py:59
  28.0 34.6 %collective-permute-start.6 = (bf16[448,576]{1,0:T(8,128)(2,1)S(1)}, bf16[448,576]{1,0:T(8,128)(2,1)}, u32[]{:S(2)}, u32[]{:S(2)}) collective-permute-start(bf16[448,576]{1,0:T(8,128)(2,1)S(1)} %collective-permute-done.2), channel_id=1, source_target_pairs={{2,0},{4,2},{6,4},{7,6},{5,7},{3,5},{1,3},{0,1},{10,8},{12,10},{14... | collective-permute-start | bytes 1548296 | tf_op jit(solution)/shard_map/ppermute | solution.py:59
  28.9 36.9 %collective-permute-start.1 = (bf16[448,576]{1,0:T(8,128)(2,1)}, bf16[448,576]{1,0:T(8,128)(2,1)}, u32[]{:S(2)}, u32[]{:S(2)}) collective-permute-start(bf16[448,576]{1,0:T(8,128)(2,1)} %collective-permute-done), channel_id=1, source_target_pairs={{0,8},{8,0},{16,24},{24,16},{1,9},{9,1},{17,25},{25,17},{2,10},{10... | collective-permute-start | bytes 1548296 | tf_op jit(solution)/shard_map/ppermute | solution.py:141
  29.1 39.7 %collective-permute-start.3 = (bf16[448,576]{1,0:T(8,128)(2,1)S(1)}, bf16[448,576]{1,0:T(8,128)(2,1)}, u32[]{:S(2)}, u32[]{:S(2)}) collective-permute-start(bf16[448,576]{1,0:T(8,128)(2,1)S(1)} %collective-permute-done.2), channel_id=1, source_target_pairs={{0,8},{8,0},{16,24},{24,16},{1,9},{9,1},{17,25},{25,17},{2,10},{10... | collective-permute-start | bytes 1548296 | tf_op jit(solution)/shard_map/ppermute | solution.py:141
  47.3 24.0 %collective-permute-start.8 = (bf16[448,576]{1,0:T(8,128)(2,1)}, bf16[448,576]{1,0:T(8,128)(2,1)S(1)}, u32[]{:S(2)}, u32[]{:S(2)}) collective-permute-start(bf16[448,576]{1,0:T(8,128)(2,1)} %collective-permute-done.4), channel_id=1, source_target_pairs={{0,2},{2,4},{4,6},{6,7},{7,5},{5,3},{3,1},{1,0},{8,10},{10,12},{12... | collective-permute-start | bytes 1548296 | tf_op jit(solution)/shard_map/ppermute | solution.py:59
  62.6 20.4 %collective-permute-start.5 = (bf16[448,576]{1,0:T(8,128)(2,1)}, bf16[448,576]{1,0:T(8,128)(2,1)S(1)}, u32[]{:S(2)}, u32[]{:S(2)}) collective-permute-start(bf16[448,576]{1,0:T(8,128)(2,1)} %collective-permute-done.4), channel_id=1, source_target_pairs={{0,8},{8,0},{16,24},{24,16},{1,9},{9,1},{17,25},{25,17},{2,10},{10... | collective-permute-start | bytes 1548296 | tf_op jit(solution)/shard_map/ppermute | solution.py:141
  62.7 17.9 %collective-permute-start.10 = (bf16[448,576]{1,0:T(8,128)(2,1)}, bf16[448,576]{1,0:T(8,128)(2,1)S(1)}, u32[]{:S(2)}, u32[]{:S(2)}) collective-permute-start(bf16[448,576]{1,0:T(8,128)(2,1)} %collective-permute-done.6), channel_id=1, source_target_pairs={{2,0},{4,2},{6,4},{7,6},{5,7},{3,5},{1,3},{0,1},{10,8},{12,10},{14... | collective-permute-start | bytes 1548296 | tf_op jit(solution)/shard_map/ppermute | solution.py:59
  65.9 20.0 %collective-permute-start.7 = (bf16[448,576]{1,0:T(8,128)(2,1)}, bf16[448,576]{1,0:T(8,128)(2,1)S(1)}, u32[]{:S(2)}, u32[]{:S(2)}) collective-permute-start(bf16[448,576]{1,0:T(8,128)(2,1)} %collective-permute-done.6), channel_id=1, source_target_pairs={{0,8},{8,0},{16,24},{24,16},{1,9},{9,1},{17,25},{25,17},{2,10},{10... | collective-permute-start | bytes 1548296 | tf_op jit(solution)/shard_map/ppermute | solution.py:141
  71.3 19.1 %collective-permute-start.9 = (bf16[448,576]{1,0:T(8,128)(2,1)S(1)}, bf16[448,576]{1,0:T(8,128)(2,1)S(1)}, u32[]{:S(2)}, u32[]{:S(2)}) collective-permute-start(bf16[448,576]{1,0:T(8,128)(2,1)S(1)} %collective-permute-done.8), channel_id=1, source_target_pairs={{0,8},{8,0},{16,24},{24,16},{1,9},{9,1},{17,25},{25,17},{2,10},{10... | collective-permute-start | bytes 1548296 | tf_op jit(solution)/shard_map/ppermute | solution.py:141
  73.7 13.9 %collective-permute-start.12 = (bf16[224,576]{1,0:T(8,128)(2,1)S(1)}, bf16[224,576]{1,0:T(8,128)(2,1)S(1)}, u32[]{:S(2)}, u32[]{:S(2)}) collective-permute-start(bf16[224,576]{1,0:T(8,128)(2,1)S(1)} %slice.121), channel_id=1, source_target_pairs={{0,2},{2,4},{4,6},{6,7},{7,5},{5,3},{3,1},{1,0},{8,10},{10,12},{12... | collective-permute-start | bytes 774152 | tf_op jit(solution)/shard_map/ppermute | solution.py:59
  80.6 9.8 %collective-permute-start.14 = (bf16[224,576]{1,0:T(8,128)(2,1)S(1)}, bf16[224,576]{1,0:T(8,128)(2,1)S(1)}, u32[]{:S(2)}, u32[]{:S(2)}) collective-permute-start(bf16[224,576]{1,0:T(8,128)(2,1)S(1)} %slice.122), channel_id=1, source_target_pairs={{2,0},{4,2},{6,4},{7,6},{5,7},{3,5},{1,3},{0,1},{10,8},{12,10},{14... | collective-permute-start | bytes 774152 | tf_op jit(solution)/shard_map/ppermute | solution.py:59
  83.0 9.1 %collective-permute-start.11 = (bf16[448,576]{1,0:T(8,128)(2,1)S(1)}, bf16[448,576]{1,0:T(8,128)(2,1)S(1)}, u32[]{:S(2)}, u32[]{:S(2)}) collective-permute-start(bf16[448,576]{1,0:T(8,128)(2,1)S(1)} %collective-permute-done.10), channel_id=1, source_target_pairs={{0,8},{8,0},{16,24},{24,16},{1,9},{9,1},{17,25},{25,17},{2,10},{10... | collective-permute-start | bytes 1548296 | tf_op jit(solution)/shard_map/ppermute | solution.py:141
  109.1 15.3 %collective-permute-start.17 = (bf16[512,576]{0,1:T(8,128)(2,1)S(1)}, bf16[512,576]{0,1:T(8,128)(2,1)S(1)}, u32[]{:S(2)}, u32[]{:S(2)}) collective-permute-start(bf16[512,576]{0,1:T(8,128)(2,1)S(1)} %broadcast_select_fusion), channel_id=1, source_target_pairs={{0,16},{8,24},{16,0},{24,8},{1,17},{9,25},{17,1},{25,9},{2,18},{10... | collective-permute-start | bytes 1769480 | tf_op jit(solution)/shard_map/ppermute | solution.py:195
  124.7 47.4 %collective-permute-start.18 = (bf16[512,576]{0,1:T(8,128)(2,1)S(1)}, bf16[512,576]{0,1:T(8,128)(2,1)}, u32[]{:S(2)}, u32[]{:S(2)}) collective-permute-start(bf16[512,576]{0,1:T(8,128)(2,1)S(1)} %select_select_fusion), channel_id=1, source_target_pairs={{0,2},{2,4},{4,6},{6,7},{7,5},{5,3},{3,1},{1,0},{8,10},{10,12},{12... | collective-permute-start | bytes 1769480 | tf_op jit(solution)/shard_map/ppermute | solution.py:59
  168.2 14.3 %collective-permute-start.19 = (bf16[512,576]{0,1:T(8,128)(2,1)S(1)}, bf16[512,576]{0,1:T(8,128)(2,1)}, u32[]{:S(2)}, u32[]{:S(2)}) collective-permute-start(bf16[512,576]{0,1:T(8,128)(2,1)S(1)} %select_select_fusion), channel_id=1, source_target_pairs={{2,0},{4,2},{6,4},{7,6},{5,7},{3,5},{1,3},{0,1},{10,8},{12,10},{14... | collective-permute-start | bytes 1769480 | tf_op jit(solution)/shard_map/ppermute | solution.py:59
  172.2 15.0 %collective-permute-start.20 = (bf16[512,576]{0,1:T(8,128)(2,1)}, bf16[512,576]{0,1:T(8,128)(2,1)}, u32[]{:S(2)}, u32[]{:S(2)}) collective-permute-start(bf16[512,576]{0,1:T(8,128)(2,1)} %collective-permute-done.18), channel_id=1, source_target_pairs={{0,2},{2,4},{4,6},{6,7},{7,5},{5,3},{3,1},{1,0},{8,10},{10,12},{12... | collective-permute-start | bytes 1769480 | tf_op jit(solution)/shard_map/ppermute | solution.py:59
  182.4 15.3 %collective-permute-start.21 = (bf16[512,576]{0,1:T(8,128)(2,1)}, bf16[512,576]{0,1:T(8,128)(2,1)}, u32[]{:S(2)}, u32[]{:S(2)}) collective-permute-start(bf16[512,576]{0,1:T(8,128)(2,1)} %collective-permute-done.19), channel_id=1, source_target_pairs={{2,0},{4,2},{6,4},{7,6},{5,7},{3,5},{1,3},{0,1},{10,8},{12,10},{14... | collective-permute-start | bytes 1769480 | tf_op jit(solution)/shard_map/ppermute | solution.py:59
  187.2 22.4 %collective-permute-start.22 = (bf16[512,576]{0,1:T(8,128)(2,1)}, bf16[512,576]{0,1:T(8,128)(2,1)S(1)}, u32[]{:S(2)}, u32[]{:S(2)}) collective-permute-start(bf16[512,576]{0,1:T(8,128)(2,1)} %collective-permute-done.20), channel_id=1, source_target_pairs={{0,2},{2,4},{4,6},{6,7},{7,5},{5,3},{3,1},{1,0},{8,10},{10,12},{12... | collective-permute-start | bytes 1769480 | tf_op jit(solution)/shard_map/ppermute | solution.py:59
  197.7 14.8 %collective-permute-start.23 = (bf16[512,576]{0,1:T(8,128)(2,1)}, bf16[512,576]{0,1:T(8,128)(2,1)S(1)}, u32[]{:S(2)}, u32[]{:S(2)}) collective-permute-start(bf16[512,576]{0,1:T(8,128)(2,1)} %collective-permute-done.21), channel_id=1, source_target_pairs={{2,0},{4,2},{6,4},{7,6},{5,7},{3,5},{1,3},{0,1},{10,8},{12,10},{14... | collective-permute-start | bytes 1769480 | tf_op jit(solution)/shard_map/ppermute | solution.py:59
  253.5 7.3 %collective-permute-start.26 = (bf16[128,448]{1,0:T(8,128)(2,1)S(1)}, bf16[128,448]{1,0:T(8,128)(2,1)S(1)}, u32[]{:S(2)}, u32[]{:S(2)}) collective-permute-start(bf16[128,448]{1,0:T(8,128)(2,1)S(1)} %get-tuple-element.11), channel_id=1, source_target_pairs={{0,2},{2,4},{4,6},{6,7},{7,5},{5,3},{3,1},{1,0},{8,10},{10,12},{12... | collective-permute-start | bytes 344072 | tf_op jit(solution)/shard_map/ppermute | solution.py:59
  261.0 7.3 %collective-permute-start.27 = (bf16[128,896]{1,0:T(8,128)(2,1)S(1)}, bf16[128,896]{1,0:T(8,128)(2,1)S(1)}, u32[]{:S(2)}, u32[]{:S(2)}) collective-permute-start(bf16[128,896]{1,0:T(8,128)(2,1)S(1)} %pad_maximum_fusion.3), channel_id=1, source_target_pairs={{0,2},{2,4},{4,6},{6,7},{7,5},{5,3},{3,1},{1,0},{8,10},{10,12},{12... | collective-permute-start | bytes 688136 | tf_op jit(solution)/shard_map/ppermute | solution.py:59
  (31 other events, 564.7 us)
Sparse Core Ops, SparseCore 0:
  17.5 69.3 reduce-scatter.1
